TPU v7x, 32 devices: a whole 2x2x4 slice. The times are simulated.
32 devices in a mesh: row: 8 (over z, x), col: 4 (over y, core).
Axes of the slice: x: 2, y: 2, z: 4, core: 2. Of those that a mesh axis runs over, the one named last changes fastest.
Arguments:
- eigvecs: float32 [2048, 65536], P(('col', 'row')), may hold values from -6 to 6
- reflectors: float32 [4, 256, 65536], P(None, 'col', 'row'), may hold values from -0.0234375 to 0.0234375
- tfactors: float32 [4, 256, 256], replicated, may hold values from -0.5 to 2, as said below
Outputs:
- backed: float32 [65536, 2048], P('row', 'col')
Inputs may be any that keep to these rules, and one draw needn't show every extreme that they name: `tfactors`: each block's factor is upper triangular with diagonal entries between 1 and 2.
All inputs are finite; a program needn't handle non-finite values.
Results may differ from a plain program's by a relative error of at most 0.0001.
Values sent between devices are 32-bit elements; how exact they have to be, the bound alone decides.
A program may use at most 128 MiB of HBM per device.

v0:
```python
import jax
import jax.numpy as jnp
from jax import lax
from jax.sharding import PartitionSpec as P


def matmul(left, right):
    return jnp.dot(left, right, precision=lax.Precision.HIGHEST, preferred_element_type=jnp.float32)


def inner_rows(left, right):
    return lax.dot_general(
        left,
        right,
        (((0,), (0,)), ((), ())),
        precision=lax.Precision.HIGHEST,
        preferred_element_type=jnp.float32,
    )


def body(eigvecs, reflectors, tfactors):
    arrived = lax.all_to_all(eigvecs, "row", split_axis=1, concat_axis=0, tiled=True)
    current = arrived.T
    blocks = tfactors.shape[0]
    for block in range(blocks - 1, -1, -1):
        vectors = lax.all_gather(reflectors[block], "col", axis=0, tiled=True)
        inner_part = matmul(vectors, current)
        inner_sum = lax.psum(inner_part, "row")
        scaled = matmul(tfactors[block], inner_sum)
        current = current - inner_rows(vectors, scaled)
    return current


def solution(mesh):
    in_specs = (P(("col", "row"), None), P(None, "col", "row"), P())
    out_specs = P("row", "col")
    return jax.shard_map(body, mesh=mesh, in_specs=in_specs, out_specs=out_specs, check_vma=False)
```

profile of v0, /device:TPU:0, one launch (start us, length us, event | category | flops | bytes accessed | tf_op | source)
XLA Modules:
  0.0 982.3 jit_solution(12616680192022693570)
XLA Ops:
  6.5 11.7 %copy.8 = f32[8,8,8,8192]{3,2,0,1:T(8,128)} copy(f32[8,8,8,8192]{3,2,1,0:T(8,128)} %bitcast.66) | data formatting | bytes 33554432 | tf_op jit(solution)/shard_map/all_to_all | solution.py:22
  18.2 7.3 all-to-all-start
  25.5 6.9 fusion.33
  32.5 59.8 %all-gather.9.cloned.1.call-done = f32[1,256,8192]{2,1,0:T(8,128)} async-done(((f32[1,64,8192]{2,1,0:T(8,128)}), f32[1,256,8192]{2,1,0:T(8,128)}) %all-gather.9.cloned.1.call-update) | async-done | bytes 8388624 | tf_op jit(solution)/shard_map/all_gather | solution.py:26
  92.3 296.3 %all-to-all-done = f32[64,8,8192]{2,0,1:T(8,128)} async-done(((f32[64,8,8192]{2,0,1:T(8,128)}), f32[64,8,8192]{2,0,1:T(8,128)}, u32[]{:S(2)}, u32[]{:S(2)}) %all-to-all-start) | async-done | bytes 16777248 | tf_op jit(solution)/shard_map/all_to_all | solution.py:22
  388.5 19.4 %fusion.10 = f32[256,512]{1,0:T(8,128)} fusion(f32[512,8192]{1,0:T(8,128)} %bitcast.1, f32[1,256,8192]{2,1,0:T(8,128)} %all-gather.9.cloned.1.call-done), kind=kOutput, calls=%fused_computation.15 | convolution fusion | flops 12884901888 | bytes 25690112 | tf_op jit(solution)/shard_map/dot_general | solution.py:8
  409.3 70.2 %all-reduce.5.cloned.1.call-done = f32[256,512]{1,0:T(8,128)} async-done(((f32[256,512]{1,0:T(8,128)}), f32[256,512]{1,0:T(8,128)}) %all-reduce.5.cloned.1.call-update) | async-done | bytes 524304 | tf_op jit(solution)/shard_map/psum | solution.py:28
  479.6 2.0 fusion.27
  481.6 25.9 %convolution_subtract_fusion.2 = f32[512,8192]{1,0:T(8,128)} fusion(f32[512,8192]{1,0:T(8,128)} %bitcast.1, f32[512,256]{1,0:T(8,128)S(1)} %fusion.27, f32[1,256,8192]{2,1,0:T(8,128)} %all-gather.9.cloned.1.call-done), kind=kOutput, calls=%fused_computation.4 | convolution fusion | flops 12889096192 | bytes 42467328 | tf_op jit(solution)/shard_map/dot_general | solution.py:12
  507.5 31.3 %all-gather.11.cloned.1.call-done = f32[1,256,8192]{2,1,0:T(8,128)} async-done(((f32[1,64,8192]{2,1,0:T(8,128)}), f32[1,256,8192]{2,1,0:T(8,128)}) %all-gather.11.cloned.1.call-update) | async-done | bytes 8388624 | tf_op jit(solution)/shard_map/all_gather | solution.py:26
  538.8 18.4 %fusion.12 = f32[256,512]{0,1:T(8,128)} fusion(f32[512,8192]{1,0:T(8,128)} %convolution_subtract_fusion.2, f32[1,256,8192]{2,1,0:T(8,128)} %all-gather.11.cloned.1.call-done), kind=kOutput, calls=%fused_computation.17 | convolution fusion | flops 12884901888 | bytes 25690112 | tf_op jit(solution)/shard_map/dot_general | solution.py:8
  558.1 71.7 %all-reduce.7.cloned.1.call-done = f32[256,512]{0,1:T(8,128)} async-done(((f32[256,512]{0,1:T(8,128)}), f32[256,512]{0,1:T(8,128)}) %all-reduce.7.cloned.1.call-update) | async-done | bytes 524304 | tf_op jit(solution)/shard_map/psum | solution.py:28
  629.8 1.7 fusion.25
  631.5 25.9 %convolution_subtract_fusion.1 = f32[512,8192]{1,0:T(8,128)} fusion(f32[512,8192]{1,0:T(8,128)} %convolution_subtract_fusion.2, f32[512,256]{1,0:T(8,128)S(1)} %fusion.25, f32[1,256,8192]{2,1,0:T(8,128)} %all-gather.11.cloned.1.call-done), kind=kOutput, calls=%fused_computation.3 | convolution fusion | flops 12889096192 | bytes 42467328 | tf_op jit(solution)/shard_map/dot_general | solution.py:12
  657.4 31.4 %all-gather.13.cloned.1.call-done = f32[1,256,8192]{2,1,0:T(8,128)} async-done(((f32[1,64,8192]{2,1,0:T(8,128)}), f32[1,256,8192]{2,1,0:T(8,128)}) %all-gather.13.cloned.1.call-update) | async-done | bytes 8388624 | tf_op jit(solution)/shard_map/all_gather | solution.py:26
  688.8 18.4 %fusion.15 = f32[256,512]{0,1:T(8,128)} fusion(f32[512,8192]{1,0:T(8,128)} %convolution_subtract_fusion.1, f32[1,256,8192]{2,1,0:T(8,128)} %all-gather.13.cloned.1.call-done), kind=kOutput, calls=%fused_computation.18 | convolution fusion | flops 12884901888 | bytes 25690112 | tf_op jit(solution)/shard_map/dot_general | solution.py:8
  708.3 71.5 %all-reduce.9.cloned.1.call-done = f32[256,512]{0,1:T(8,128)} async-done(((f32[256,512]{0,1:T(8,128)}), f32[256,512]{0,1:T(8,128)}) %all-reduce.9.cloned.1.call-update) | async-done | bytes 524304 | tf_op jit(solution)/shard_map/psum | solution.py:28
  779.8 1.7 fusion.23
  781.5 25.9 %convolution_subtract_fusion = f32[512,8192]{1,0:T(8,128)} fusion(f32[512,8192]{1,0:T(8,128)} %convolution_subtract_fusion.1, f32[512,256]{1,0:T(8,128)S(1)} %fusion.23, f32[1,256,8192]{2,1,0:T(8,128)} %all-gather.13.cloned.1.call-done), kind=kOutput, calls=%fused_computation.2 | convolution fusion | flops 12889096192 | bytes 42467328 | tf_op jit(solution)/shard_map/dot_general | solution.py:12
  807.4 31.7 %all-gather.15.cloned.1.call-done = f32[1,256,8192]{2,1,0:T(8,128)} async-done(((f32[1,64,8192]{2,1,0:T(8,128)}), f32[1,256,8192]{2,1,0:T(8,128)}) %all-gather.15.cloned.1.call-update) | async-done | bytes 8388624 | tf_op jit(solution)/shard_map/all_gather | solution.py:26
  839.0 18.4 %fusion.18 = f32[256,512]{0,1:T(8,128)} fusion(f32[512,8192]{1,0:T(8,128)} %convolution_subtract_fusion, f32[1,256,8192]{2,1,0:T(8,128)} %all-gather.15.cloned.1.call-done), kind=kOutput, calls=%fused_computation.19 | convolution fusion | flops 12884901888 | bytes 25690112 | tf_op jit(solution)/shard_map/dot_general | solution.py:8
  857.5 72.5 %all-reduce.11.cloned.1.call-done = f32[256,512]{0,1:T(8,128)} async-done(((f32[256,512]{0,1:T(8,128)}), f32[256,512]{0,1:T(8,128)}) %all-reduce.11.cloned.1.call-update) | async-done | bytes 524304 | tf_op jit(solution)/shard_map/psum | solution.py:28
  931.7 26.1 %subtract_bitcast_fusion = f32[8192,512]{0,1:T(8,128)} fusion(f32[512,8192]{1,0:T(8,128)} %convolution_subtract_fusion, f32[512,256]{1,0:T(8,128)S(1)} %fusion.21, f32[1,256,8192]{2,1,0:T(8,128)} %all-gather.15.cloned.1.call-done), kind=kOutput, calls=%fused_computation.1 | convolution fusion | flops 12889096192 | bytes 42467328 | tf_op jit(solution)/shard_map/dot_general | solution.py:12
  957.7 17.4 %copy.5 = f32[8192,512]{1,0:T(8,128)} copy(f32[8192,512]{0,1:T(8,128)} %subtract_bitcast_fusion) | data formatting | bytes 33554432 | tf_op jit(solution)/shard_map/sub | solution.py:30
  (19 shorter events, 4.9 us)
Async XLA Ops:
  18.2 370.3 %all-to-all-start = ((f32[64,8,8192]{2,0,1:T(8,128)}), f32[64,8,8192]{2,0,1:T(8,128)}, u32[]{:S(2)}, u32[]{:S(2)}) async-start(f32[64,8,8192]{2,0,1:T(8,128)} %bitcast.65), calls=%async_computation | async-start | bytes 33554432 | tf_op jit(solution)/shard_map/all_to_all | solution.py:22
  25.5 66.8 %all-gather.9.cloned.1.call-start = ((), (), s32[]{:S(2)}) async-start(), calls=%async_computation.5 | async-start | bytes 10485760 | tf_op jit(solution)/shard_map/all_gather | solution.py:26
  32.4 447.1 %all-reduce.5.cloned.1.call-start = ((), (), s32[]{:S(2)}) async-start(), calls=%async_computation.1 | async-start | bytes 1048576 | tf_op jit(solution)/shard_map/psum | solution.py:28
  388.5 91.0 %copy-start = (f32[4,256,256]{2,1,0:T(8,128)S(1)}, f32[4,256,256]{2,1,0:T(8,128)}, u32[]{:S(2)}) copy-start(f32[4,256,256]{2,1,0:T(8,128)} %param.5) | copy-start | bytes 3145732
  408.0 130.8 %all-gather.11.cloned.1.call-start = ((), (), s32[]{:S(2)}) async-start(), calls=%async_computation.6 | async-start | bytes 10485760 | tf_op jit(solution)/shard_map/all_gather | solution.py:26
  408.7 221.0 %all-reduce.7.cloned.1.call-start = ((), (), s32[]{:S(2)}) async-start(), calls=%async_computation.2 | async-start | bytes 1048576 | tf_op jit(solution)/shard_map/psum | solution.py:28
  557.3 131.5 %all-gather.13.cloned.1.call-start = ((), (), s32[]{:S(2)}) async-start(), calls=%async_computation.7 | async-start | bytes 10485760 | tf_op jit(solution)/shard_map/all_gather | solution.py:26
  557.8 221.9 %all-reduce.9.cloned.1.call-start = ((), (), s32[]{:S(2)}) async-start(), calls=%async_computation.3 | async-start | bytes 1048576 | tf_op jit(solution)/shard_map/psum | solution.py:28
  707.3 131.8 %all-gather.15.cloned.1.call-start = ((), (), s32[]{:S(2)}) async-start(), calls=%async_computation.8 | async-start | bytes 10485760 | tf_op jit(solution)/shard_map/all_gather | solution.py:26
  708.0 222.0 %all-reduce.11.cloned.1.call-start = ((), (), s32[]{:S(2)}) async-start(), calls=%async_computation.4 | async-start | bytes 1048576 | tf_op jit(solution)/shard_map/psum | solution.py:28
Sparse Core Ops, SparseCore 0:
  32.6 59.6 all-gather.8
  408.1 71.3 all-reduce.4
  481.2 57.5 all-gather.10
  557.4 72.3 all-reduce.6
  631.2 57.5 all-gather.12
  707.4 72.3 all-reduce.8
  781.4 57.5 all-gather.14
  857.6 72.3 all-reduce.10
where the time goes:
time: 988 us; the launch traced here: 982 us
  waiting for transfers between devices  738 us (75%)
  matrix products  185 us (19%)
  local copies, waits for them, and re-layouts  36 us (4%)
  between operations  13.8 us (1%)
    all_to_all x1, waiting for transfers between devices, body(): lax.all_to_all(eigvecs, 'row', split_axis=1, concat_axis=0, tiled=True)  296 us
    psum x4, waiting for transfers between devices, body(): inner_sum = lax.psum(inner_part, 'row')  286 us
    all_gather x4, waiting for transfers between devices, body(): vectors = lax.all_gather(reflectors[block], 'col', axis=0, tiled=True)  154 us
    dot_general x4, matrix products, inner_rows(): lax.dot_general(left, right, (((0,), (0,)), ((), ())), precision=lax.Prec...  104 us
    dot_general x8, matrix products, matmul(): jnp.dot(left, right, precision=lax.Precision.HIGHEST, preferred_element_t...  81.7 us
  transfers between devices with their start and end apart: 9, of which 9 were waited for; matrix products, arithmetic and copies ran while one was open for 9% of the time, Pallas kernels for 0%

commit v1 on v0

--- a/solution.py
+++ b/solution.py
@@ -23,7 +23,14 @@
     current = arrived.T
     blocks = tfactors.shape[0]
     for block in range(blocks - 1, -1, -1):
-        vectors = lax.all_gather(reflectors[block], "col", axis=0, tiled=True)
+        ring = [reflectors[block]]
+        for hop in range(3):
+            ring.append(lax.ppermute(ring[-1], "col", [(dev, (dev + 1) % 4) for dev in range(4)]))
+        vectors = jnp.roll(
+            jnp.concatenate(ring[::-1], axis=0),
+            (lax.axis_index("col") + 1) * ring[0].shape[0],
+            axis=0,
+        )
         inner_part = matmul(vectors, current)
         inner_sum = lax.psum(inner_part, "row")
         scaled = matmul(tfactors[block], inner_sum)

time: 988 us -> 912 us (0.923)
  waiting for transfers between devices: 738 us -> 581 us
  other arithmetic: 0 us -> 45 us
  matrix products: 185 us -> 221 us
    ppermute x0 -> x12, waiting for transfers between devices: none -> 203 us  [body(): lax.ppermute(ring[-1], 'col', [(dev, (dev + 1) % 4) for dev in range(4)])]
    all_gather x4 -> x0, waiting for transfers between devices: 154 us -> none  [body(): vectors = lax.all_gather(reflectors[block], 'col', axis=0, tiled=True)]
    all_to_all x1, waiting for transfers between devices: 296 us -> 143 us  [body(): lax.all_to_all(eigvecs, 'row', split_axis=1, concat_axis=0, tiled=True)]
    psum x4, waiting for transfers between devices: 286 us -> 235 us  [body(): inner_sum = lax.psum(inner_part, 'row')]
    concatenate x0 -> x4, other arithmetic: none -> 45 us  [body(): jnp.roll(jnp.concatenate(ring[::-1], axis=0), (lax.axis_index('col') + 1)...]
    dot_general x4, matrix products: 104 us -> 140 us  [inner_rows(): lax.dot_general(left, right, (((0,), (0,)), ((), ())), precision=lax.Prec...]
    all_to_all x1 -> x2, local copies, waits for them, and re-layouts: 11.7 us -> 29.2 us  [body(): lax.all_to_all(eigvecs, 'row', split_axis=1, concat_axis=0, tiled=True)]
    sub x1 -> x0, local copies, waits for them, and re-layouts: 17.4 us -> none  [body(): current = current - inner_rows(vectors, scaled)]
  transfers between devices with their start and end apart: 9 -> 17, of which waited for: 9 -> 14; matrix products, arithmetic and copies ran while one was open for 9% -> 22% of each run, Pallas kernels for 0% -> 0%
where the time goes in v1:
time: 912 us; the launch traced here: 904 us
  waiting for transfers between devices  581 us (64%)
  matrix products  221 us (24%)
  other arithmetic  45 us (5%)
  local copies, waits for them, and re-layouts  33.3 us (4%)
  between operations  13.7 us (2%)
  starting transfers between devices  10.1 us (1%)
    psum x4, waiting for transfers between devices, body(): inner_sum = lax.psum(inner_part, 'row')  235 us
    ppermute x12, waiting for transfers between devices, body(): lax.ppermute(ring[-1], 'col', [(dev, (dev + 1) % 4) for dev in range(4)])  203 us
    all_to_all x1, waiting for transfers between devices, body(): lax.all_to_all(eigvecs, 'row', split_axis=1, concat_axis=0, tiled=True)  143 us
    dot_general x4, matrix products, inner_rows(): lax.dot_general(left, right, (((0,), (0,)), ((), ())), precision=lax.Prec...  140 us
    dot_general x8, matrix products, matmul(): jnp.dot(left, right, precision=lax.Precision.HIGHEST, preferred_element_t...  81 us
    concatenate x4, other arithmetic, body(): jnp.roll(jnp.concatenate(ring[::-1], axis=0), (lax.axis_index('col') + 1)...  45 us
    all_to_all x2, local copies, waits for them, and re-layouts, body(): lax.all_to_all(eigvecs, 'row', split_axis=1, concat_axis=0, tiled=True)  29.2 us
  transfers between devices with their start and end apart: 17, of which 14 were waited for; matrix products, arithmetic and copies ran while one was open for 22% of the time, Pallas kernels for 0%

profile of v1, /device:TPU:0, one launch (start us, length us, event | category | flops | bytes accessed | tf_op | source)
XLA Modules:
  0.0 904.0 jit_solution(12188512367301289373)
XLA Ops:
  31.9 23.2 %collective-permute-done = f32[64,8192]{1,0:T(8,128)S(1)} collective-permute-done((f32[64,8192]{1,0:T(8,128)S(1)}, f32[64,8192]{1,0:T(8,128)S(1)}, u32[]{:S(2)}, u32[]{:S(2)}) %collective-permute-start) | collective-permute-done | bytes 2097184 | tf_op jit(solution)/shard_map/ppermute | solution.py:28
  55.1 22.6 %collective-permute-done.3 = f32[64,8192]{1,0:T(8,128)} collective-permute-done((f32[64,8192]{1,0:T(8,128)S(1)}, f32[64,8192]{1,0:T(8,128)}, u32[]{:S(2)}, u32[]{:S(2)}) %collective-permute-start.3) | collective-permute-done | bytes 2097184 | tf_op jit(solution)/shard_map/ppermute | solution.py:28
  77.7 22.5 %collective-permute-done.6 = f32[64,8192]{1,0:T(8,128)} collective-permute-done((f32[64,8192]{1,0:T(8,128)S(1)}, f32[64,8192]{1,0:T(8,128)}, u32[]{:S(2)}, u32[]{:S(2)}) %collective-permute-start.6) | collective-permute-done | bytes 2097184 | tf_op jit(solution)/shard_map/ppermute | solution.py:28
  100.2 22.5 %collective-permute-done.9 = f32[64,8192]{1,0:T(8,128)} collective-permute-done((f32[64,8192]{1,0:T(8,128)S(1)}, f32[64,8192]{1,0:T(8,128)}, u32[]{:S(2)}, u32[]{:S(2)}) %collective-permute-start.9) | collective-permute-done | bytes 2097184 | tf_op jit(solution)/shard_map/ppermute | solution.py:28
  122.6 22.5 %collective-permute-done.1 = f32[64,8192]{1,0:T(8,128)} collective-permute-done((f32[64,8192]{1,0:T(8,128)S(1)}, f32[64,8192]{1,0:T(8,128)}, u32[]{:S(2)}, u32[]{:S(2)}) %collective-permute-start.1) | collective-permute-done | bytes 2097184 | tf_op jit(solution)/shard_map/ppermute | solution.py:28
  145.1 22.5 %collective-permute-done.4 = f32[64,8192]{1,0:T(8,128)} collective-permute-done((f32[64,8192]{1,0:T(8,128)}, f32[64,8192]{1,0:T(8,128)}, u32[]{:S(2)}, u32[]{:S(2)}) %collective-permute-start.4) | collective-permute-done | bytes 2097184 | tf_op jit(solution)/shard_map/ppermute | solution.py:28
  167.6 22.5 %collective-permute-done.7 = f32[64,8192]{1,0:T(8,128)} collective-permute-done((f32[64,8192]{1,0:T(8,128)}, f32[64,8192]{1,0:T(8,128)}, u32[]{:S(2)}, u32[]{:S(2)}) %collective-permute-start.7) | collective-permute-done | bytes 2097184 | tf_op jit(solution)/shard_map/ppermute | solution.py:28
  190.1 22.5 %collective-permute-done.10 = f32[64,8192]{1,0:T(8,128)} collective-permute-done((f32[64,8192]{1,0:T(8,128)}, f32[64,8192]{1,0:T(8,128)}, u32[]{:S(2)}, u32[]{:S(2)}) %collective-permute-start.10) | collective-permute-done | bytes 2097184 | tf_op jit(solution)/shard_map/ppermute | solution.py:28
  212.5 22.5 %collective-permute-done.2 = f32[64,8192]{1,0:T(8,128)} collective-permute-done((f32[64,8192]{1,0:T(8,128)}, f32[64,8192]{1,0:T(8,128)}, u32[]{:S(2)}, u32[]{:S(2)}) %collective-permute-start.2) | collective-permute-done | bytes 2097184 | tf_op jit(solution)/shard_map/ppermute | solution.py:28
  245.9 142.6 %all-to-all-done = f32[64,8,8192]{2,0,1:T(8,128)} async-done(((f32[64,8,8192]{2,0,1:T(8,128)}), f32[64,8,8192]{2,0,1:T(8,128)}, u32[]{:S(2)}, u32[]{:S(2)}) %all-to-all-start) | async-done | bytes 16777248 | tf_op jit(solution)/shard_map/all_to_all | solution.py:22
  388.5 19.4 %fusion.40 = f32[256,512]{1,0:T(8,128)} fusion(f32[256,8192]{1,0:T(8,128)} %fusion.24, f32[512,8192]{1,0:T(8,128)} %bitcast.1), kind=kOutput, calls=%fused_computation.81 | convolution fusion | flops 12884901888 | bytes 25690112 | tf_op jit(solution)/shard_map/dot_general | solution.py:8
  408.3 12.1 %fusion.17 = f32[256,8192]{1,0:T(8,128)} fusion(s32[]{:T(128)S(6)} %select_n.17, f32[64,8192]{1,0:T(8,128)} %collective-permute-done.5, f32[64,8192]{1,0:T(8,128)} %collective-permute-done.4, f32[64,8192]{1,0:T(8,128)} %collective-permute-done.3, f32[64,8192]{1,0:T(8,128)S(1)} %get-tuple-element.7), kind=kLoop, calls=%fused_computation.54 | loop fusion | flops 14680064 | bytes 16777220 | tf_op jit(solution)/shard_map/jit(_roll_dynamic)/concatenate | solution.py:29
  420.4 17.5 %copy.9 = f32[512,8192]{0,1:T(8,128)} copy(f32[512,8192]{1,0:T(8,128)} %bitcast.1) | data formatting | bytes 33554432 | tf_op jit(solution)/shard_map/all_to_all | solution.py:22
  437.9 41.6 %all-reduce.5.cloned.1.call-done = f32[256,512]{1,0:T(8,128)} async-done(((f32[256,512]{1,0:T(8,128)}), f32[256,512]{1,0:T(8,128)}) %all-reduce.5.cloned.1.call-update) | async-done | bytes 524304 | tf_op jit(solution)/shard_map/psum | solution.py:35
  481.8 35.0 %bitcast_subtract_fusion = f32[8192,512]{1,0:T(8,128)} fusion(f32[512,8192]{0,1:T(8,128)} %copy.9, f32[256,8192]{1,0:T(8,128)} %fusion.24, f32[512,256]{1,0:T(8,128)S(1)} %fusion.34), kind=kOutput, calls=%fused_computation.33 | convolution fusion | flops 12889096192 | bytes 42467328 | tf_op jit(solution)/shard_map/dot_general | solution.py:12
  516.8 17.6 %fusion.41 = f32[256,512]{1,0:T(8,128)} fusion(f32[256,8192]{1,0:T(8,128)S(1)} %bitcast.50, f32[8192,512]{1,0:T(8,128)} %bitcast_subtract_fusion), kind=kOutput, calls=%fused_computation.82 | convolution fusion | flops 12884901888 | bytes 25690112 | tf_op jit(solution)/shard_map/dot_general | solution.py:8
  545.4 60.8 %all-reduce.7.cloned.1.call-done = f32[256,512]{1,0:T(8,128)} async-done(((f32[256,512]{1,0:T(8,128)}), f32[256,512]{1,0:T(8,128)}) %all-reduce.7.cloned.1.call-update) | async-done | bytes 524304 | tf_op jit(solution)/shard_map/psum | solution.py:35
  608.5 35.5 %convolution_subtract_fusion.2 = f32[8192,512]{1,0:T(8,128)} fusion(f32[8192,512]{1,0:T(8,128)} %bitcast_subtract_fusion, f32[256,8192]{1,0:T(8,128)} %fusion.17, f32[512,256]{1,0:T(8,128)S(1)} %fusion.32), kind=kOutput, calls=%fused_computation.36 | convolution fusion | flops 12889096192 | bytes 42467328 | tf_op jit(solution)/shard_map/dot_general | solution.py:12
  644.0 17.6 %fusion.42 = f32[256,512]{1,0:T(8,128)} fusion(f32[256,8192]{1,0:T(8,128)S(1)} %bitcast.52, f32[8192,512]{1,0:T(8,128)} %convolution_subtract_fusion.2), kind=kOutput, calls=%fused_computation.83 | convolution fusion | flops 12884901888 | bytes 25690112 | tf_op jit(solution)/shard_map/dot_general | solution.py:8
  672.6 60.8 %all-reduce.9.cloned.1.call-done = f32[256,512]{1,0:T(8,128)} async-done(((f32[256,512]{1,0:T(8,128)}), f32[256,512]{1,0:T(8,128)}) %all-reduce.9.cloned.1.call-update) | async-done | bytes 524304 | tf_op jit(solution)/shard_map/psum | solution.py:35
  735.7 35.0 %convolution_subtract_fusion.1 = f32[8192,512]{1,0:T(8,128)} fusion(f32[8192,512]{1,0:T(8,128)} %convolution_subtract_fusion.2, f32[256,8192]{1,0:T(8,128)} %fusion.10, f32[512,256]{1,0:T(8,128)S(1)} %fusion.30), kind=kOutput, calls=%fused_computation.35 | convolution fusion | flops 12889096192 | bytes 42467328 | tf_op jit(solution)/shard_map/dot_general | solution.py:12
  770.7 17.6 %fusion.43 = f32[256,512]{1,0:T(8,128)} fusion(f32[256,8192]{1,0:T(8,128)S(1)} %bitcast.54, f32[8192,512]{1,0:T(8,128)} %convolution_subtract_fusion.1), kind=kOutput, calls=%fused_computation.84 | convolution fusion | flops 12884901888 | bytes 25690112 | tf_op jit(solution)/shard_map/dot_general | solution.py:8
  788.3 71.8 %all-reduce.11.cloned.1.call-done = f32[256,512]{1,0:T(8,128)} async-done(((f32[256,512]{1,0:T(8,128)}), f32[256,512]{1,0:T(8,128)}) %all-reduce.11.cloned.1.call-update) | async-done | bytes 524304 | tf_op jit(solution)/shard_map/psum | solution.py:35
  862.2 34.9 %convolution_subtract_fusion = f32[8192,512]{1,0:T(8,128)} fusion(f32[8192,512]{1,0:T(8,128)} %convolution_subtract_fusion.1, f32[256,8192]{1,0:T(8,128)} %fusion.3, f32[512,256]{1,0:T(8,128)S(1)} %fusion.28), kind=kOutput, calls=%fused_computation.34 | convolution fusion | flops 12889096192 | bytes 42467328 | tf_op jit(solution)/shard_map/dot_general | solution.py:12
  (56 shorter events, 67.7 us)
Async XLA Ops:
  18.2 370.3 %all-to-all-start = ((f32[64,8,8192]{2,0,1:T(8,128)}), f32[64,8,8192]{2,0,1:T(8,128)}, u32[]{:S(2)}, u32[]{:S(2)}) async-start(f32[64,8,8192]{2,0,1:T(8,128)} %bitcast.55), calls=%async_computation | async-start | bytes 33554432 | tf_op jit(solution)/shard_map/all_to_all | solution.py:22
  25.5 454.1 %all-reduce.5.cloned.1.call-start = ((), (), s32[]{:S(2)}) async-start(), calls=%async_computation.1 | async-start | bytes 1048576 | tf_op jit(solution)/shard_map/psum | solution.py:35
  29.6 93.1 %copy-start.1 = (f32[64,8192]{1,0:T(8,128)}, f32[64,8192]{1,0:T(8,128)S(1)}, u32[]{:S(2)}) copy-start(f32[64,8192]{1,0:T(8,128)S(1)} %get-tuple-element.9) | copy-start | bytes 6291460
  29.6 93.0 %copy-start.2 = (f32[64,8192]{1,0:T(8,128)}, f32[64,8192]{1,0:T(8,128)S(1)}, u32[]{:S(2)}) copy-start(f32[64,8192]{1,0:T(8,128)S(1)} %get-tuple-element.8) | copy-start | bytes 6291460
  29.6 25.5 %collective-permute-start = (f32[64,8192]{1,0:T(8,128)S(1)}, f32[64,8192]{1,0:T(8,128)S(1)}, u32[]{:S(2)}, u32[]{:S(2)}) collective-permute-start(f32[64,8192]{1,0:T(8,128)S(1)} %get-tuple-element.8), channel_id=1, source_target_pairs={{0,1},{1,2},{2,3},{3,0},{4,5},{5,6},{6,7},{7,4},{8,9},{9,10},{10,1... | collective-permute-start | bytes 6291464 | tf_op jit(solution)/shard_map/ppermute | solution.py:28
  29.7 48.0 %collective-permute-start.3 = (f32[64,8192]{1,0:T(8,128)S(1)}, f32[64,8192]{1,0:T(8,128)}, u32[]{:S(2)}, u32[]{:S(2)}) collective-permute-start(f32[64,8192]{1,0:T(8,128)S(1)} %get-tuple-element.7), channel_id=1, source_target_pairs={{0,1},{1,2},{2,3},{3,0},{4,5},{5,6},{6,7},{7,4},{8,9},{9,10},{10,1... | collective-permute-start | bytes 6291464 | tf_op jit(solution)/shard_map/ppermute | solution.py:28
  31.3 68.9 %collective-permute-start.6 = (f32[64,8192]{1,0:T(8,128)S(1)}, f32[64,8192]{1,0:T(8,128)}, u32[]{:S(2)}, u32[]{:S(2)}) collective-permute-start(f32[64,8192]{1,0:T(8,128)S(1)} %get-tuple-element.9), channel_id=1, source_target_pairs={{0,1},{1,2},{2,3},{3,0},{4,5},{5,6},{6,7},{7,4},{8,9},{9,10},{10,1... | collective-permute-start | bytes 6291464 | tf_op jit(solution)/shard_map/ppermute | solution.py:28
  31.4 91.3 %collective-permute-start.9 = (f32[64,8192]{1,0:T(8,128)S(1)}, f32[64,8192]{1,0:T(8,128)}, u32[]{:S(2)}, u32[]{:S(2)}) collective-permute-start(f32[64,8192]{1,0:T(8,128)S(1)} %get-tuple-element.6), channel_id=1, source_target_pairs={{0,1},{1,2},{2,3},{3,0},{4,5},{5,6},{6,7},{7,4},{8,9},{9,10},{10,1... | collective-permute-start | bytes 6291464 | tf_op jit(solution)/shard_map/ppermute | solution.py:28
  55.1 90.0 %copy-start.3 = (f32[64,8192]{1,0:T(8,128)}, f32[64,8192]{1,0:T(8,128)S(1)}, u32[]{:S(2)}) copy-start(f32[64,8192]{1,0:T(8,128)S(1)} %collective-permute-done) | copy-start | bytes 6291460
  55.1 90.0 %collective-permute-start.1 = (f32[64,8192]{1,0:T(8,128)S(1)}, f32[64,8192]{1,0:T(8,128)}, u32[]{:S(2)}, u32[]{:S(2)}) collective-permute-start(f32[64,8192]{1,0:T(8,128)S(1)} %collective-permute-done), channel_id=1, source_target_pairs={{0,1},{1,2},{2,3},{3,0},{4,5},{5,6},{6,7},{7,4},{8,9},{9,10},{10,1... | collective-permute-start | bytes 6291464 | tf_op jit(solution)/shard_map/ppermute | solution.py:28
  77.7 89.9 %collective-permute-start.4 = (f32[64,8192]{1,0:T(8,128)}, f32[64,8192]{1,0:T(8,128)}, u32[]{:S(2)}, u32[]{:S(2)}) collective-permute-start(f32[64,8192]{1,0:T(8,128)} %collective-permute-done.3), channel_id=1, source_target_pairs={{0,1},{1,2},{2,3},{3,0},{4,5},{5,6},{6,7},{7,4},{8,9},{9,10},{10,1... | collective-permute-start | bytes 6291464 | tf_op jit(solution)/shard_map/ppermute | solution.py:28
  100.2 89.9 %collective-permute-start.7 = (f32[64,8192]{1,0:T(8,128)}, f32[64,8192]{1,0:T(8,128)}, u32[]{:S(2)}, u32[]{:S(2)}) collective-permute-start(f32[64,8192]{1,0:T(8,128)} %collective-permute-done.6), channel_id=1, source_target_pairs={{0,1},{1,2},{2,3},{3,0},{4,5},{5,6},{6,7},{7,4},{8,9},{9,10},{10,1... | collective-permute-start | bytes 6291464 | tf_op jit(solution)/shard_map/ppermute | solution.py:28
  122.6 89.9 %collective-permute-start.10 = (f32[64,8192]{1,0:T(8,128)}, f32[64,8192]{1,0:T(8,128)}, u32[]{:S(2)}, u32[]{:S(2)}) collective-permute-start(f32[64,8192]{1,0:T(8,128)} %collective-permute-done.9), channel_id=1, source_target_pairs={{0,1},{1,2},{2,3},{3,0},{4,5},{5,6},{6,7},{7,4},{8,9},{9,10},{10,1... | collective-permute-start | bytes 6291464 | tf_op jit(solution)/shard_map/ppermute | solution.py:28
  145.1 89.9 %collective-permute-start.2 = (f32[64,8192]{1,0:T(8,128)}, f32[64,8192]{1,0:T(8,128)}, u32[]{:S(2)}, u32[]{:S(2)}) collective-permute-start(f32[64,8192]{1,0:T(8,128)} %collective-permute-done.1), channel_id=1, source_target_pairs={{0,1},{1,2},{2,3},{3,0},{4,5},{5,6},{6,7},{7,4},{8,9},{9,10},{10,1... | collective-permute-start | bytes 6291464 | tf_op jit(solution)/shard_map/ppermute | solution.py:28
  167.6 240.7 %collective-permute-start.5 = (f32[64,8192]{1,0:T(8,128)}, f32[64,8192]{1,0:T(8,128)}, u32[]{:S(2)}, u32[]{:S(2)}) collective-permute-start(f32[64,8192]{1,0:T(8,128)} %collective-permute-done.4), channel_id=1, source_target_pairs={{0,1},{1,2},{2,3},{3,0},{4,5},{5,6},{6,7},{7,4},{8,9},{9,10},{10,1... | collective-permute-start | bytes 6291464 | tf_op jit(solution)/shard_map/ppermute | solution.py:28
  190.1 344.4 %collective-permute-start.8 = (f32[64,8192]{1,0:T(8,128)}, f32[64,8192]{1,0:T(8,128)}, u32[]{:S(2)}, u32[]{:S(2)}) collective-permute-start(f32[64,8192]{1,0:T(8,128)} %collective-permute-done.7), channel_id=1, source_target_pairs={{0,1},{1,2},{2,3},{3,0},{4,5},{5,6},{6,7},{7,4},{8,9},{9,10},{10,1... | collective-permute-start | bytes 6291464 | tf_op jit(solution)/shard_map/ppermute | solution.py:28
  212.5 449.1 %collective-permute-start.11 = (f32[64,8192]{1,0:T(8,128)}, f32[64,8192]{1,0:T(8,128)}, u32[]{:S(2)}, u32[]{:S(2)}) collective-permute-start(f32[64,8192]{1,0:T(8,128)} %collective-permute-done.10), channel_id=1, source_target_pairs={{0,1},{1,2},{2,3},{3,0},{4,5},{5,6},{6,7},{7,4},{8,9},{9,10},{10,1... | collective-permute-start | bytes 6291464 | tf_op jit(solution)/shard_map/ppermute | solution.py:28
  407.9 198.3 %all-reduce.7.cloned.1.call-start = ((), (), s32[]{:S(2)}) async-start(), calls=%async_computation.2 | async-start | bytes 1048576 | tf_op jit(solution)/shard_map/psum | solution.py:35
  479.5 37.2 %slice-start = ((s8[8388608]{0:T(1024)(128)(4,1)}), s8[4194304]{0:T(1024)(128)(4,1)S(1)}, s32[]{:S(2)}) async-start(s8[8388608]{0:T(1024)(128)(4,1)} %bitcast.49), calls=%async_computation.5 | async-start | bytes 8388608
  534.4 199.0 %all-reduce.9.cloned.1.call-start = ((), (), s32[]{:S(2)}) async-start(), calls=%async_computation.3 | async-start | bytes 1048576 | tf_op jit(solution)/shard_map/psum | solution.py:35
  606.2 37.7 %slice-start.2 = ((s8[8388608]{0:T(1024)(128)(4,1)}), s8[4194304]{0:T(1024)(128)(4,1)S(1)}, s32[]{:S(2)}) async-start(s8[8388608]{0:T(1024)(128)(4,1)} %bitcast.51), calls=%async_computation.7 | async-start | bytes 8388608
  608.5 35.5 %slice-start.3 = ((s8[8388608]{0:T(1024)(128)(4,1)}), s8[4194304]{0:T(1024)(128)(4,1)S(1)}, s32[]{:S(2)}) async-start(s8[8388608]{0:T(1024)(128)(4,1)} %bitcast.51), calls=%async_computation.8 | async-start | bytes 8388608
  661.6 198.5 %all-reduce.11.cloned.1.call-start = ((), (), s32[]{:S(2)}) async-start(), calls=%async_computation.4 | async-start | bytes 1048576 | tf_op jit(solution)/shard_map/psum | solution.py:35
  733.4 37.3 %slice-start.4 = ((s8[8388608]{0:T(1024)(128)(4,1)}), s8[4194304]{0:T(1024)(128)(4,1)S(1)}, s32[]{:S(2)}) async-start(s8[8388608]{0:T(1024)(128)(4,1)} %bitcast.53), calls=%async_computation.9 | async-start | bytes 8388608
  (3 other events, 71.8 us)
Sparse Core Ops, SparseCore 0:
  408.0 71.4 all-reduce.4
  534.5 71.6 all-reduce.6
  661.7 71.6 all-reduce.8
  788.4 71.6 all-reduce.10
